TPU v7x, 256 devices: a whole 4x4x8 slice. The times are simulated.
256 devices in a mesh: mem: 32 (over x, z), cell: 8 (over y, core).
Axes of the slice: x: 4, y: 4, z: 8, core: 2. Of those that a mesh axis runs over, the one named last changes fastest.
Arguments:
- prior_states: bfloat16 [128, 4194304], P('mem', 'cell'), may hold values from -6 to 6
- measured_anomalies: bfloat16 [8, 256, 256, 128], P('cell', 'mem'), may hold values from -6 to 6
- departure_from_mean: bfloat16 [8, 256, 256], P('cell', 'mem'), may hold values from -6 to 6
- inverse_error_variance: bfloat16 [8, 256, 256], P('cell', 'mem'), may hold values from 0.25 to 4
- region_segment_indices: int32 [8, 256, 8], P('cell'), may hold values from 0 to 255, as said below
- active_slot_tallies: int32 [8, 256], P('cell'), may hold values from 4 to 8
- localization_coefficient: float32 [8, 256, 8], P('cell', 'mem'), may hold values from 0.2 to 1
Outputs:
- analysis: bfloat16 [128, 4194304], P('mem', 'cell')
Inputs may be any that keep to these rules, and one draw needn't show every extreme that they name: `region_segment_indices`: entries index blocks of the patch's own cell block. Over the 8 patches i = m * 8 to m * 8 + 7 of one cell block taken together, the entries with one value of entry // 8 number at most 3, and exactly 3 for one such value.
All inputs are finite; a program needn't handle non-finite values.
Results may differ from a plain program's by a relative error of at most 0.006.
Values may be sent and summed in bfloat16 or wider, within the bound.
A program may use at most 128 MiB of HBM per device.

v0:
```python
import math

import jax
import jax.numpy as jnp
from jax import lax
from jax.sharding import PartitionSpec as P

ITERS = 4


HIGHEST = lax.Precision.HIGHEST


def body(
    prior_states,
    measured_anomalies,
    departure_from_mean,
    inverse_error_variance,
    region_segment_indices,
    active_slot_tallies,
    localization_coefficient,
):
    point_clusters = lax.axis_size("mem")
    my_index = lax.axis_index("mem")
    region_sequence = localization_coefficient.shape[1]
    nlist = localization_coefficient.shape[2]
    per_block = measured_anomalies.shape[2]
    realization_sequence = prior_states.shape[0] * point_clusters
    mesh_points = prior_states.shape[1] // (point_clusters * region_sequence)
    requests = region_sequence * nlist
    gathered_lines = lax.all_to_all(prior_states, "mem", split_axis=1, concat_axis=0, tiled=True)
    own_lists = lax.dynamic_slice_in_dim(
        region_segment_indices[0], my_index * region_sequence, region_sequence, 0
    )
    own_counts = lax.dynamic_slice_in_dim(
        active_slot_tallies[0], my_index * region_sequence, region_sequence, 0
    )
    wanted = own_lists.reshape(requests)
    all_obs, all_innov, all_prec = (
        lax.all_gather(measured_anomalies, "mem", axis=1, tiled=True),
        lax.all_gather(departure_from_mean, "mem", axis=1, tiled=True),
        lax.all_gather(inverse_error_variance, "mem", axis=1, tiled=True),
    )
    picked = all_obs[0][wanted]
    values = all_innov[0][wanted]
    scales = all_prec[0][wanted]
    picked = picked.reshape(region_sequence, nlist, per_block, realization_sequence)
    values = values.reshape(region_sequence, nlist, per_block)
    scales = scales.reshape(region_sequence, nlist, per_block).astype(jnp.float32)
    active = (jnp.arange(nlist)[None, :] < own_counts[:, None]).astype(jnp.float32)
    weights = (localization_coefficient[0] * active)[:, :, None] * scales
    power_here = jnp.sum(weights * jnp.square(values.astype(jnp.float32)))
    squares = jnp.einsum("psok,psok->pso", picked, picked, preferred_element_type=jnp.float32)
    spread_here = jnp.sum(weights * squares) / (realization_sequence - 1)
    power_sum, spread_sum = lax.psum((power_here, spread_here), ("mem", "cell"))
    variance_scaling_factor = power_sum / spread_sum
    rows = nlist * per_block
    weighted = (
        (picked.astype(jnp.float32) * weights[:, :, :, None])
        .astype(jnp.bfloat16)
        .reshape(region_sequence, rows, realization_sequence)
    )
    flat_obs = picked.reshape(region_sequence, rows, realization_sequence)
    gram_matrix = jnp.einsum("plk,plj->pkj", weighted, flat_obs, preferred_element_type=jnp.float32)
    projected = jnp.einsum(
        "pl,plk->pk",
        values.reshape(region_sequence, rows),
        weighted,
        preferred_element_type=jnp.float32,
    )
    identity = jnp.eye(realization_sequence, dtype=jnp.float32)
    system = (realization_sequence - 1) / variance_scaling_factor * identity[None] + gram_matrix
    level = jnp.sqrt(jnp.sum(system * system, axis=(1, 2)))
    approach = system / level[:, None, None]
    inverse_root = jnp.broadcast_to(identity, system.shape)
    for sweep in range(ITERS):
        factor = 1.5 * identity[None] - 0.5 * jnp.einsum(
            "pij,pjk->pik", inverse_root, approach, precision=HIGHEST
        )
        approach = jnp.einsum("pij,pjk->pik", approach, factor, precision=HIGHEST)
        inverse_root = jnp.einsum("pij,pjk->pik", factor, inverse_root, precision=HIGHEST)
    root = inverse_root / jnp.sqrt(level)[:, None, None]
    inner_step = jnp.einsum("pij,pj->pi", root, projected, precision=HIGHEST)
    mean_shift = jnp.einsum("pij,pj->pi", root, inner_step, precision=HIGHEST)
    transform = (math.sqrt(realization_sequence - 1) * root + mean_shift[:, :, None]).astype(
        jnp.bfloat16
    )
    members_here = gathered_lines.reshape(realization_sequence, region_sequence, mesh_points)
    means = jnp.mean(members_here.astype(jnp.float32), axis=0)
    deviation = (members_here.astype(jnp.float32) - means[None]).astype(jnp.bfloat16)
    updated = means[None] + jnp.einsum(
        "pjk,jpc->kpc", transform, deviation, preferred_element_type=jnp.float32
    )
    updated = updated.astype(jnp.bfloat16).reshape(
        realization_sequence, region_sequence * mesh_points
    )
    return lax.all_to_all(updated, "mem", split_axis=0, concat_axis=1, tiled=True)


def solution(mesh):
    return jax.shard_map(
        body,
        mesh=mesh,
        in_specs=(
            P("mem", "cell"),
            P("cell", "mem", None, None),
            P("cell", "mem", None),
            P("cell", "mem", None),
            P("cell", None, None),
            P("cell", None),
            P("cell", "mem", None),
        ),
        out_specs=P("mem", "cell"),
        check_vma=False,
    )
```

profile of v0, /device:TPU:2, one launch (start us, length us, event | category | flops | bytes accessed | tf_op | source)
XLA Modules:
  0.0 490.4 jit_solution(976014501808879999)
XLA Ops:
  6.5 0.0 copy-start
  6.5 0.0 all-gather.2.cloned.1.call-start
  6.5 0.7 all-gather.2.cloned.1.call-update
  7.3 0.0 copy-start.4
  7.3 0.0 copy-start.7
  7.3 0.0 copy-start.5
  7.3 0.0 copy-start.6
  7.3 11.8 %all-to-all-start = ((bf16[4,32,16384]{2,0,1:T(4,128)(2,1)}), bf16[4,32,16384]{2,0,1:T(4,128)(2,1)}, u32[]{:S(2)}, u32[]{:S(2)}) async-start(bf16[4,32,16384]{2,0,1:T(4,128)(2,1)} %bitcast.71), calls=%async_computation | async-start | bytes 8388608 | tf_op jit(solution)/shard_map/all_to_all | solution.py:31
  19.1 0.0 copy-done.4
  19.1 0.1 squeeze.19
  19.2 0.0 copy-done.7
  19.2 0.1 dynamic-slice_bitcast_fusion
  19.3 0.1 iota_compare_fusion.1
  19.4 0.1 lt.45
  19.5 0.0 copy-done
  19.5 0.1 constant_dynamic-slice_fusion
  19.5 0.1 copy.18
  19.6 0.1 reshape.135
  19.7 0.0 copy-done.5
  19.7 154.0 %all_gather.11 = bf16[1,256,256]{2,1,0:T(8,128)(2,1)S(1)} all-gather(bf16[1,8,256]{2,1,0:T(8,128)(2,1)S(1)} %copy-done.5), channel_id=1, replica_groups=mesh['mem'=32,'cell'=8] {'mem'}, dimensions={1}, use_global_device_ids=true | all-gather | bytes 135168 | tf_op jit(solution)/shard_map/all_gather | solution.py:41
  173.7 0.7 gather_fusion.2
  174.4 0.0 copy-done.6
  174.4 41.0 %all_gather.9 = bf16[1,256,256]{2,1,0:T(8,128)(2,1)S(1)} all-gather(bf16[1,8,256]{2,1,0:T(8,128)(2,1)S(1)} %copy-done.6), channel_id=1, replica_groups=mesh['mem'=32,'cell'=8] {'mem'}, dimensions={1}, use_global_device_ids=true | all-gather | bytes 135168 | tf_op jit(solution)/shard_map/all_gather | solution.py:42
  215.4 0.7 gather_fusion
  216.2 0.8 multiply_reduce_fusion.1
  216.9 0.1 bitcast_select_fusion
  217.0 0.0 all-to-all-done
  217.0 4.1 convert_reduce_fusion
  221.1 6.4 %convert_bitcast_fusion = f32[32,4,16384]{2,1,0:T(4,128)} fusion(bf16[4,32,16384]{2,0,1:T(4,128)(2,1)} %all-to-all-done), kind=kLoop, calls=%fused_computation.3 | loop fusion | flops 2097152 | bytes 12582912 | tf_op jit(solution)/shard_map/convert_element_type | solution.py:89
  227.5 10.9 %reshape.138 = f32[128,8,2048]{2,1,0:T(8,128)} reshape(f32[32,4,16384]{2,1,0:T(4,128)} %convert_bitcast_fusion) | data formatting | bytes 16777216 | tf_op jit(solution)/shard_map/convert_element_type | solution.py:89
  238.4 6.5 %subtract_convert_fusion = bf16[128,8,2048]{2,1,0:T(8,128)(2,1)} fusion(f32[128,8,2048]{2,1,0:T(8,128)} %reshape.138, f32[8,2048]{1,0:T(8,128)S(1)} %div.33), kind=kLoop, calls=%fused_computation.9 | loop fusion | flops 4194304 | bytes 12648448 | tf_op jit(solution)/shard_map/convert_element_type | solution.py:90
  245.0 0.0 all-gather.2.cloned.1.call-done
  245.0 8.8 %gather_fusion.1 = bf16[64,256,128]{2,1,0:T(8,128)(2,1)} fusion(bf16[256,256,128]{2,1,0:T(8,128)(2,1)} %bitcast.74, s32[1024]{0:T(1024)S(1)} %pad_clamp_fusion), kind=kCustom, calls=%fused_computation.1 | custom fusion | bytes 8388864 | tf_op jit(solution)/shard_map/gather | solution.py:44
  253.8 4.4 fusion
  258.2 0.7 fusion.20
  259.5 75.5 %all-reduce = (f32[]{:T(128)}, f32[]{:T(128)}) all-reduce(f32[]{:T(128)S(6)} %div.34, f32[]{:T(128)} %multiply_reduce_fusion.1), channel_id=1, replica_groups=mesh['mem'=32,'cell'=8] {'mem','cell'}, use_global_device_ids=true, to_apply=%region_2.0 | all-reduce | flops 2 | bytes 16 | tf_op jit(solution)/shard_map/psum | solution.py:55
  336.4 6.5 %copy.20 = bf16[8,2048,128]{1,2,0:T(8,128)(2,1)} copy(bf16[8,2048,128]{2,1,0:T(8,128)(2,1)} %bitcast.68) | data formatting | bytes 8388608 | tf_op jit(solution)/shard_map/reshape | solution.py:47
  342.9 4.8 multiply_reduce_fusion
  347.7 0.7 fusion.10
  348.4 0.7 fusion.18
  349.1 0.6 fusion.15
  349.7 0.7 fusion.9
  350.4 0.0 copy-start.2
  350.4 0.7 fusion.27
  351.1 0.7 fusion.26
  351.8 0.7 fusion.8
  352.4 0.7 fusion.28
  353.1 0.7 fusion.29
  353.8 0.0 copy-done.2
  353.8 0.0 copy-start.3
  353.8 1.2 fusion.12
  355.0 0.7 fusion.7
  355.7 0.7 convolution_divide_fusion
  356.4 0.9 convolution_bitcast_fusion
  357.3 0.9 fusion.30
  358.2 0.0 copy-done.3
  358.2 8.6 %fusion.4 = bf16[128,8,2048]{0,2,1:T(8,128)(2,1)} fusion(bf16[128,8,2048]{2,1,0:T(8,128)(2,1)S(1)} %copy-done.3, f32[8,2048]{1,0:T(8,128)S(1)} %div.33, f32[8,128,128]{2,1,0:T(8,128)S(1)} %convolution_divide_fusion, f32[8,128]{1,0:T(8,128)S(1)} %bitcast.77), kind=kOutput, calls=%fused_computation.13 | convolution fusion | flops 541458432 | bytes 8982528 | tf_op jit(solution)/shard_map/pjk,jpc->kpc/dot_general | solution.py:91
  366.8 6.7 %copy.22 = bf16[128,8,2048]{2,1,0:T(8,128)(2,1)} copy(bf16[128,8,2048]{0,2,1:T(8,128)(2,1)} %fusion.4) | data formatting | bytes 8388608 | tf_op jit(solution)/shard_map/convert_element_type | solution.py:94
  373.5 7.8 %all_to_all.26 = bf16[32,4,16384]{2,1,0:T(4,128)(2,1)} reshape(bf16[128,8,2048]{2,1,0:T(8,128)(2,1)} %copy.22) | data formatting | bytes 8388608 | tf_op jit(solution)/shard_map/all_to_all | solution.py:97
  381.3 100.3 %all_to_all.32 = bf16[32,4,16384]{2,1,0:T(4,128)(2,1)S(1)} all-to-all(bf16[32,4,16384]{2,1,0:T(4,128)(2,1)} %all_to_all.26), channel_id=1, replica_groups=mesh['mem'=32,'cell'=8] {'mem'}, dimensions={0} | all-to-all | bytes 8388608 | tf_op jit(solution)/shard_map/all_to_all | solution.py:97
  481.6 0.0 copy-start.1
  481.6 2.0 copy.39
  483.6 0.0 copy-done.1
  (13 shorter events, 0.2 us)
Async XLA Ops:
  6.5 12.9 %copy-start = (s32[1,256,8]{1,2,0:T(8,128)S(1)}, s32[1,256,8]{1,2,0:T(8,128)}, u32[]{:S(2)}) copy-start(s32[1,256,8]{1,2,0:T(8,128)} %param.11) | copy-start | bytes 24580
  6.5 238.4 %all-gather.2.cloned.1.call-start = ((), (), s32[]{:S(2)}) async-start(), calls=%async_computation.2 | async-start | bytes 17301504 | tf_op jit(solution)/shard_map/all_gather | solution.py:40
  7.3 11.9 %copy-start.4 = (f32[1,8,8]{2,1,0:T(8,128)S(1)}, f32[1,8,8]{2,1,0:T(8,128)}, u32[]{:S(2)}) copy-start(f32[1,8,8]{2,1,0:T(8,128)} %param.13) | copy-start | bytes 772
  7.3 12.0 %copy-start.7 = (s32[1,256]{1,0:T(1,128)S(1)}, s32[1,256]{1,0:T(1,128)}, u32[]{:S(2)}) copy-start(s32[1,256]{1,0:T(1,128)} %param.12) | copy-start | bytes 3076
  7.3 12.4 %copy-start.5 = (bf16[1,8,256]{2,1,0:T(8,128)(2,1)S(1)}, bf16[1,8,256]{2,1,0:T(8,128)(2,1)}, u32[]{:S(2)}) copy-start(bf16[1,8,256]{2,1,0:T(8,128)(2,1)} %param.9) | copy-start | bytes 12292
  7.3 167.1 %copy-start.6 = (bf16[1,8,256]{2,1,0:T(8,128)(2,1)S(1)}, bf16[1,8,256]{2,1,0:T(8,128)(2,1)}, u32[]{:S(2)}) copy-start(bf16[1,8,256]{2,1,0:T(8,128)(2,1)} %param.10) | copy-start | bytes 12292
  7.3 209.7 %all-to-all-start = ((bf16[4,32,16384]{2,0,1:T(4,128)(2,1)}), bf16[4,32,16384]{2,0,1:T(4,128)(2,1)}, u32[]{:S(2)}, u32[]{:S(2)}) async-start(bf16[4,32,16384]{2,0,1:T(4,128)(2,1)} %bitcast.71), calls=%async_computation | async-start | bytes 8388608 | tf_op jit(solution)/shard_map/all_to_all | solution.py:31
  350.4 3.4 copy-start.2
  353.8 4.4 copy-start.3
  481.6 2.0 copy-start.1
Sparse Core Ops, SparseCore 0:
  10.0 203.2 all-gather.1
where the time goes:
time: 494 us; the launch traced here: 490 us
  blocking collectives  371 us (75%)
  local copies, waits for them, and re-layouts  44.7 us (9%)
  matrix products  23.7 us (5%)
  other arithmetic  23.1 us (5%)
  between operations  15.6 us (3%)
  starting transfers between devices  11.8 us (2%)
    all_gather x1, blocking collectives, body(): lax.all_gather(departure_from_mean, 'mem', axis=1, tiled=True)  154 us
    all_to_all x1, blocking collectives, body(): lax.all_to_all(updated, 'mem', split_axis=0, concat_axis=1, tiled=True)  100 us
    psum x1, blocking collectives, body(): power_sum, spread_sum = lax.psum((power_here, spread_here), ('mem', 'cell'))  75.5 us
    all_gather x1, blocking collectives, body(): lax.all_gather(inverse_error_variance, 'mem', axis=1, tiled=True)  41 us
    all_to_all x1, starting transfers between devices, body(): lax.all_to_all(prior_states, 'mem', split_axis=1, concat_axis=0, tiled=True)  11.8 us
    convert_element_type x1, local copies, waits for them, and re-layouts, body(): means = jnp.mean(members_here.astype(jnp.float32), axis=0)  10.9 us
  transfers between devices with their start and end apart: 2, of which 0 were waited for; matrix products, arithmetic and copies ran while one was open for 6% of the time, Pallas kernels for 0%

commit v1 on v0

v1 whole, which is shorter than its diff:
```python
import functools
import math

import jax
import jax.numpy as jnp
from jax import lax
from jax.experimental import pallas as pl
from jax.experimental.pallas import tpu as pltpu
from jax.sharding import PartitionSpec as P

ITERS = 4
WINDOW = 2
CHUNK = 256
GROUP = 4

HIGHEST = lax.Precision.HIGHEST
MESH = pl.DeviceIdType.MESH
F32 = jnp.float32
BF16 = jnp.bfloat16


def iota(shape, axis):
    return lax.broadcasted_iota(jnp.int32, shape, axis)


def split(value):
    high = value.astype(BF16)
    return high, (value - high.astype(F32)).astype(BF16)


def fold(gram):
    half = gram.shape[0] // 2
    row, lane = iota((half, 2 * half), 0), iota((half, 2 * half), 1)
    return jnp.where(lane >= row, gram[:half], pltpu.roll(gram[half:], half, 1))


def unfold(folded, diagonal):
    half = folded.shape[0]
    row, lane = iota((2 * half, 2 * half), 0), iota((2 * half, 2 * half), 1)
    both = jnp.concatenate([folded, pltpu.roll(folded, half, 1)], axis=0)
    direct = ((row < half) & (lane >= row)) | ((row >= half) & (lane >= half) & (lane < row))
    full = jnp.where(direct, both, both.T)
    return jnp.where(row == lane, diagonal, full)


def product(left, right):
    return jnp.dot(left, right, precision=HIGHEST, preferred_element_type=F32)


def transforms(grams, projections, ridge):
    size = grams[0].shape[0]
    identity = (iota((size, size), 0) == iota((size, size), 1)).astype(F32)
    systems = [ridge * identity + gram for gram in grams]
    levels = [jnp.sqrt(jnp.sum(system * system, keepdims=True)) for system in systems]
    approach = [system / level for system, level in zip(systems, levels)]
    inverse_root = [None] * len(grams)
    for sweep in range(ITERS):
        if sweep == 0:
            factor = [1.5 * identity - 0.5 * a for a in approach]
        else:
            factor = [1.5 * identity - 0.5 * product(r, a) for r, a in zip(inverse_root, approach)]
        if sweep < ITERS - 1:
            approach = [product(a, f) for a, f in zip(approach, factor)]
        inverse_root = factor if sweep == 0 else [product(f, r) for f, r in zip(factor, inverse_root)]
    result = []
    for inverse, level, projected in zip(inverse_root, levels, projections):
        root = inverse / jnp.sqrt(level)
        wide = jnp.broadcast_to(projected, (8, size))
        mean_shift = product(product(wide, root), root)[:1]
        result.append((math.sqrt(size - 1) * root + mean_shift).astype(BF16))
    return result


def kernel(
    nx, nz, ncell,
    x_ref, y_ref, d_ref, e_ref, idx_ref, tally_ref, loc_ref,
    out_ref,
    arrived, result, grams, stats, partial, cells, flat, change, dep, prec,
    in_send, in_recv, in_self, small_send, small_recv, z_send, z_recv, x_send, x_recv,
    out_send, out_recv, out_self,
):
    n = nx * nz
    me, cell = lax.axis_index("mem"), lax.axis_index("cell")
    my_x, my_z = me // nz, me % nz
    patches, _, rows, points = arrived.shape
    blocks, obs, members = y_ref.shape
    half = members // 2
    nlist = loc_ref.shape[0] // patches

    def peer(dx, dz):
        return lax.rem(my_x + dx + nx, nx) * nz + lax.rem(my_z + dz + nz, nz)

    def offset(o):
        return lax.rem(me + o, n) if isinstance(o, int) and o == 0 else peer(o // nz, o % nz)

    def remote(src, dst, ssem, rsem, to):
        return pltpu.make_async_remote_copy(
            src_ref=src, dst_ref=dst, send_sem=ssem, recv_sem=rsem, device_id=to, device_id_type=MESH
        )

    def to_all(make):
        @pl.loop(1, n)
        def _(o):
            make(peer(o // nz, o % nz)).start()

    barrier = pltpu.get_barrier_semaphore()

    @pl.loop(1, n)
    def _(o):
        pl.semaphore_signal(barrier, inc=1, device_id={"mem": peer(o // nz, o % nz)}, device_id_type=MESH)

    @pl.loop(1, ncell)
    def _(o):
        pl.semaphore_signal(barrier, inc=1, device_id={"cell": lax.rem(cell + o, ncell)}, device_id_type=MESH)

    pl.semaphore_wait(barrier, n - 1 + ncell - 1)

    def columns(owner, p):
        return pl.ds(pl.multiple_of((owner * patches + p) * points, 128), points)

    def own_in(p):
        return pltpu.make_async_copy(x_ref.at[:, columns(me, p)], arrived.at[p, me], in_self.at[p])

    def wait_in_send(p):
        whole = arrived.at[p, pl.ds(0, n - 1)]
        remote(whole, whole, in_send.at[p], in_recv.at[p], {"mem": me}).wait_send()

    def issue(p):
        if p >= WINDOW:
            wait_in_send(p - WINDOW)
        own_in(p).start()
        to_all(
            lambda r: remote(x_ref.at[:, columns(r, p)], arrived.at[p, me], in_send.at[p], in_recv.at[p], {"mem": r})
        )

    issue(0)
    issue(1)

    dep[...] = d_ref[...].astype(F32)
    prec[...] = e_ref[...].astype(F32)
    lane = iota((1, members), 1)
    diagonal_mask = iota((members, members), 0) == iota((members, members), 1)

    @pl.loop(0, blocks)
    def _(b):
        y = y_ref[b]
        e, d = prec[pl.ds(b, 1), :], dep[pl.ds(b, 1), :]
        weighted = (y.astype(F32).T * e).astype(BF16)
        gram = jnp.dot(weighted, y, preferred_element_type=F32)
        high, low = split(e * d)
        row = iota((16, obs), 0)
        pair = jnp.where(row == 0, high.astype(F32), jnp.where(row == 1, low.astype(F32), 0.0)).astype(BF16)
        projected = jnp.sum(jnp.dot(pair, y, preferred_element_type=F32), axis=0, keepdims=True)
        diagonal = jnp.sum(jnp.where(diagonal_mask, gram, 0.0), axis=0, keepdims=True)
        tail = jnp.concatenate(
            [part.astype(F32) for part in split(diagonal) + split(projected)] + [jnp.zeros((4, members), F32)], axis=0
        )
        grams[me * blocks + b] = jnp.concatenate([fold(gram), tail], axis=0).astype(BF16)
        power = jnp.sum(e * d * d, keepdims=True)
        spread = jnp.sum(diagonal, keepdims=True)
        stats[me * blocks + b] = jnp.where(lane < half, power, spread)

    mine = pl.ds(me * blocks, blocks)

    def small_copy(which, buffer, place, to):
        return remote(buffer.at[place], buffer.at[place], small_send.at[which], small_recv.at[which], to)

    def wait_small(which, buffer, length):
        whole = buffer.at[pl.ds(0, length)]
        remote(whole, whole, small_send.at[which], small_recv.at[which], {"mem": me}).wait()

    to_all(lambda r: small_copy(0, stats, mine, {"mem": r}))

    first, second = (0, blocks // 2), (blocks // 2, blocks // 2)

    def along_z(piece, part, sem, step):
        start, size = part or (0, blocks)
        ref = grams.at[pl.ds(piece * blocks + start, size)]
        return remote(ref, ref, z_send.at[sem], z_recv.at[sem], {"mem": peer(0, step)})

    def along_x(piece):
        for dx in range(1, nx):
            ref = grams.at[pl.ds(piece * blocks, blocks)]
            remote(ref, ref, x_send.at[0], x_recv.at[0], {"mem": peer(dx, 0)}).start()

    reach = nz // 2

    def forward(step):
        last = step == reach - 1
        along_z(peer(0, -step), first if last else None, step, 1).start()
        along_z(peer(0, step), second if last else None, reach + step, -1).start()

    def receive(step):
        last = step == reach
        along_z(peer(0, -step), first if last else None, step - 1, 1).wait_recv()
        along_z(peer(0, step), second if last else None, reach + step - 1, -1).wait_recv()

    forward(0)
    along_x(me)
    issue(2)

    def weight(p, s):
        active = jnp.clip(tally_ref[p] - s, 0, 1).astype(F32)
        return loc_ref[p * nlist + s] * active

    wait_small(0, stats, (n - 1) * blocks)

    def add_request(i, total):
        p, s = i // nlist, i % nlist
        return total + weight(p, s) * stats[idx_ref[i]]

    share = lax.fori_loop(0, patches * nlist, add_request, jnp.zeros((1, members), F32))
    mine_partial = pl.ds(pl.multiple_of(me * 8, 8), 8)
    partial[mine_partial, :] = jnp.where(iota((8, members), 0) == 0, share, 0.0)
    to_all(lambda r: small_copy(1, partial, mine_partial, {"mem": r}))

    receive(1)
    forward(1)
    along_x(peer(0, -1))
    along_x(peer(0, 1))
    issue(3)

    wait_small(1, partial, (n - 1) * 8)
    mine_cell = pl.ds(pl.multiple_of(cell * 8, 8), 8)
    group_sum = jnp.sum(partial[...], axis=0, keepdims=True)
    cells[mine_cell, :] = jnp.where(iota((8, members), 0) == 0, group_sum, 0.0)

    @pl.loop(1, ncell)
    def _(o):
        small_copy(2, cells, mine_cell, {"cell": lax.rem(cell + o, ncell)}).start()

    receive(2)
    forward(2)
    along_x(peer(0, -2))
    along_x(peer(0, 2))
    issue(4)
    receive(3)
    forward(3)
    along_x(peer(0, -3))
    along_x(peer(0, 3))
    issue(5)
    receive(4)
    along_x(peer(0, 4))
    issue(6)

    wait_small(2, cells, (ncell - 1) * 8)
    sums = jnp.sum(cells[...], axis=0, keepdims=True)
    power = jnp.sum(jnp.where(lane == 0, sums, 0.0), keepdims=True)
    spread = jnp.sum(jnp.where(lane == half, sums, 0.0), keepdims=True) / (members - 1)
    ridge = (members - 1) / (power / spread)

    issue(7)
    from_x = grams.at[pl.ds(0, nz * (nx - 1) * blocks)]
    remote(from_x, from_x, x_send.at[0], x_recv.at[0], {"mem": me}).wait()
    for step in range(reach):
        last = step == reach - 1
        along_z(peer(0, -step), first if last else None, step, 1).wait_send()
        along_z(peer(0, step), second if last else None, reach + step, -1).wait_send()

    def collect(p):
        def add(s, total):
            return total + weight(p, s) * grams[idx_ref[p * nlist + s]].astype(F32)

        total = lax.fori_loop(0, nlist, add, jnp.zeros(grams.shape[1:], F32))
        gram, diagonal = total[:half], total[half : half + 1] + total[half + 1 : half + 2]
        projected = total[half + 2 : half + 3] + total[half + 3 : half + 4]
        return unfold(gram, diagonal), projected

    @pl.loop(0, patches // GROUP)
    def _(g):
        pairs = [collect(g * GROUP + k) for k in range(GROUP)]
        made = transforms([a for a, _ in pairs], [b for _, b in pairs], ridge)
        for k in range(GROUP):
            change[g * GROUP + k] = made[k]

    @pl.loop(0, patches)
    def _(p):
        whole = arrived.at[p, pl.ds(0, n - 1)]
        remote(whole, whole, in_send.at[p], in_recv.at[p], {"mem": me}).wait_recv()
        own_in(p).wait()

        @pl.loop(0, points // CHUNK)
        def _(c):
            cut = pl.ds(pl.multiple_of(c * CHUNK, CHUNK), CHUNK)
            for m in range(n):
                flat[rows * m : rows * (m + 1), :] = arrived[p, m, :, cut].astype(F32)
            states = flat[...]
            means = jnp.sum(states, axis=0, keepdims=True) * (1.0 / members)
            deviation = (states - means).astype(BF16)
            updated = means + jnp.dot(change[p], deviation, preferred_element_type=F32)
            for m in range(n):
                result[p, m, :, cut] = updated[rows * m : rows * (m + 1), :].astype(BF16)

        pltpu.make_async_copy(result.at[p, me], out_ref.at[:, columns(me, p)], out_self.at[0]).start()
        to_all(
            lambda r: remote(
                result.at[p, r], out_ref.at[:, columns(me, p)], out_send.at[0], out_recv.at[0], {"mem": r}
            )
        )

    for p in range(patches - WINDOW, patches):
        wait_in_send(p)
    mine_out = pl.ds(pl.multiple_of(me * patches * points, 128), patches * points)
    pltpu.make_async_copy(out_ref.at[:, mine_out], out_ref.at[:, mine_out], out_self.at[0]).wait()
    others = out_ref.at[:, pl.ds(0, (n - 1) * patches * points)]
    remote(others, others, out_send.at[0], out_recv.at[0], {"mem": me}).wait()


def body(nx, nz, ncell, prior_states, anomalies, departure, precision, lists, tallies, localization):
    n = nx * nz
    me = lax.axis_index("mem")
    rows, cells = prior_states.shape
    patches, nlist = localization.shape[1:]
    points = cells // (n * patches)
    blocks, obs, members = anomalies.shape[1:]
    own_lists = lax.dynamic_slice_in_dim(lists[0], me * patches, patches, 0).reshape(-1)
    own_counts = lax.dynamic_slice_in_dim(tallies[0], me * patches, patches, 0)
    vmem, smem, anywhere = (pl.BlockSpec(memory_space=s) for s in (pltpu.VMEM, pltpu.SMEM, pl.ANY))
    dma = pltpu.SemaphoreType.DMA
    return pl.pallas_call(
        functools.partial(kernel, nx, nz, ncell),
        out_shape=jax.ShapeDtypeStruct((rows, cells), BF16),
        in_specs=[anywhere, vmem, vmem, vmem, smem, smem, smem],
        out_specs=anywhere,
        scratch_shapes=[
            pltpu.VMEM((patches, n, rows, points), BF16),
            pltpu.VMEM((patches, n, rows, points), BF16),
            pltpu.VMEM((n * blocks, members // 2 + 8, members), BF16),
            pltpu.VMEM((n * blocks, 1, members), F32),
            pltpu.VMEM((n * 8, members), F32),
            pltpu.VMEM((ncell * 8, members), F32),
            pltpu.VMEM((members, CHUNK), F32),
            pltpu.VMEM((patches, members, members), BF16),
            pltpu.VMEM((blocks, obs), F32),
            pltpu.VMEM((blocks, obs), F32),
            dma((patches,)),
            dma((patches,)),
            dma((patches,)),
            dma((3,)),
            dma((3,)),
            dma((nz,)),
            dma((nz,)),
            dma((1,)),
            dma((1,)),
            dma((1,)),
            dma((1,)),
            dma((1,)),
        ],
        compiler_params=pltpu.CompilerParams(
            collective_id=0, has_side_effects=True, vmem_limit_bytes=56 * 2**20
        ),
        name="analysis_kernel",
    )(
        prior_states, anomalies[0], departure[0], precision[0], own_lists, own_counts, localization[0].reshape(-1)
    )


def solution(mesh):
    nx, nz = 4, mesh.shape["mem"] // 4
    return jax.shard_map(
        functools.partial(body, nx, nz, mesh.shape["cell"]),
        mesh=mesh,
        in_specs=(
            P("mem", "cell"),
            P("cell", "mem", None, None),
            P("cell", "mem", None),
            P("cell", "mem", None),
            P("cell", None, None),
            P("cell", None),
            P("cell", "mem", None),
        ),
        out_specs=P("mem", "cell"),
        check_vma=False,
    )
```

time: 494 us -> 231 us (0.47)
  blocking collectives: 371 us -> 0 us
  Pallas kernels: 0 us -> 220 us
  local copies, waits for them, and re-layouts: 44.7 us -> 8.66 us
  matrix products: 23.7 us -> 0 us
  other arithmetic: 23.1 us -> 0 us
  between operations: 15.6 us -> 0.01 us
  starting transfers between devices: 11.8 us -> 0 us
    pallas_call x0 -> x1, Pallas kernels: none -> 220 us  [body(): pl.pallas_call(functools.partial(kernel, nx, nz, ncell), out_shape=jax.Sh...]
    all_gather x2 -> x0, blocking collectives: 195 us -> none  [the longest x1 154 us: body(): lax.all_gather(departure_from_mean, 'mem', axis=1, tiled=True)]
    all_to_all x1 -> x0, blocking collectives: 100 us -> none  [body(): lax.all_to_all(updated, 'mem', split_axis=0, concat_axis=1, tiled=True)]
    psum x1 -> x0, blocking collectives: 75.5 us -> none  [body(): power_sum, spread_sum = lax.psum((power_here, spread_here), ('mem', 'cell'))]
    dot_general x16 -> x0, matrix products: 23.7 us -> none  [the longest x1 8.57 us: body(): jnp.einsum('pjk,jpc->kpc', transform, deviation, preferred_element_type=j...]
    convert_element_type x3 -> x0, local copies, waits for them, and re-layouts: 17.6 us -> none  [the longest x1 10.9 us: body(): means = jnp.mean(members_here.astype(jnp.float32), axis=0)]
    convert_element_type x3 -> x0, other arithmetic: 13 us -> none  [the longest x1 6.55 us: body(): (members_here.astype(jnp.float32) - means[None]).astype(jnp.bfloat16)]
    all_to_all x1 -> x0, starting transfers between devices: 11.8 us -> none  [body(): lax.all_to_all(prior_states, 'mem', split_axis=1, concat_axis=0, tiled=True)]
  transfers between devices with their start and end apart: 2 -> 0, of which waited for: 0 -> 0; matrix products, arithmetic and copies ran while one was open for 6% -> 0% of each run, Pallas kernels for 0% -> 0%
where the time goes in v1:
time: 231 us; the launch traced here: 228 us
  Pallas kernels  220 us (95%)
  local copies, waits for them, and re-layouts  8.66 us (4%)
    pallas_call x1, Pallas kernels, body(): pl.pallas_call(functools.partial(kernel, nx, nz, ncell), out_shape=jax.Sh...  220 us
    unnamed x3, local copies, waits for them, and re-layouts  5.29 us

profile of v1, /device:TPU:2, one launch (start us, length us, event | category | flops | bytes accessed | tf_op | source)
XLA Modules:
  0.0 228.4 jit_solution(15755731308868212522)
XLA Ops:
  0.0 0.0 copy-start
  0.0 1.3 dynamic-slice_bitcast_fusion.tally_ref
  1.3 1.4 reshape_squeeze.3.loc_ref
  2.6 0.0 copy-done
  2.6 0.1 constant_dynamic-slice_fusion
  2.7 0.1 copy.8
  2.8 0.6 reshape.6.idx_ref
  3.4 219.8 %analysis_kernel.1 = bf16[4,524288]{1,0:T(4,128)(2,1)} custom-call(bf16[4,524288]{1,0:T(4,128)(2,1)} %x_ref.1, bf16[8,256,128]{2,1,0:T(8,128)(2,1)} %bitcast.5, bf16[8,256]{1,0:T(8,128)(2,1)} %bitcast.6, bf16[8,256]{1,0:T(8,128)(2,1)} %bitcast.7, s32[64]{0:T(128)} %reshape.6.idx_ref, s32[8]{0:T(128)} %dynamic-slice_bitcast_fusion.tally_ref, ...), custom_call_target="tpu_custom_call" | custom-call | tf_op jit(solution)/shard_map/analysis_kernel/pallas_call | solution.py:320
  223.2 5.3 %copy.10 = bf16[4,524288]{1,0:T(4,128)(2,1)} copy(bf16[4,524288]{1,0:T(4,128)(2,1)} %analysis_kernel.1) | data formatting | bytes 8388608
Async XLA Ops:
  0.0 2.6 %copy-start = (s32[1,256,8]{1,2,0:T(8,128)S(1)}, s32[1,256,8]{1,2,0:T(8,128)}, u32[]{:S(2)}) copy-start(s32[1,256,8]{1,2,0:T(8,128)} %param.11) | copy-start | bytes 24580

commit v2 on v1

v2 whole, which is shorter than its diff:
```python
import functools
import math

import jax
import jax.numpy as jnp
from jax import lax
from jax.experimental import pallas as pl
from jax.experimental.pallas import tpu as pltpu
from jax.sharding import PartitionSpec as P

ITERS = 4
WINDOW = 6
PACE = 4
BATCH = 8
CHUNK = 256
GROUP = 4

HIGHEST = lax.Precision.HIGHEST
MESH = pl.DeviceIdType.MESH
F32 = jnp.float32
BF16 = jnp.bfloat16


def iota(shape, axis):
    return lax.broadcasted_iota(jnp.int32, shape, axis)


def split(value):
    high = value.astype(BF16)
    return high, (value - high.astype(F32)).astype(BF16)


def fold(gram):
    half = gram.shape[0] // 2
    row, lane = iota((half, 2 * half), 0), iota((half, 2 * half), 1)
    return jnp.where(lane >= row, gram[:half], pltpu.roll(gram[half:], half, 1))


def unfold(folded, diagonal):
    half = folded.shape[0]
    row, lane = iota((2 * half, 2 * half), 0), iota((2 * half, 2 * half), 1)
    both = jnp.concatenate([folded, pltpu.roll(folded, half, 1)], axis=0)
    direct = ((row < half) & (lane >= row)) | ((row >= half) & (lane >= half) & (lane < row))
    full = jnp.where(direct, both, both.T)
    return jnp.where(row == lane, diagonal, full)


def with_tail(folded, diagonal, projected):
    parts = split(diagonal) + split(projected)
    rows = [part.astype(F32) for part in parts] + [jnp.zeros((4, folded.shape[1]), F32)]
    return jnp.concatenate([folded] + rows, axis=0).astype(BF16)


def from_tail(whole):
    half = whole.shape[0] - 8
    row = [whole[half + k : half + k + 1] for k in range(4)]
    return whole[:half], row[0] + row[1], row[2] + row[3]


def product(left, right):
    return jnp.dot(left, right, precision=HIGHEST, preferred_element_type=F32)


def transforms(grams, projections, ridge):
    size = grams[0].shape[0]
    identity = (iota((size, size), 0) == iota((size, size), 1)).astype(F32)
    systems = [ridge * identity + gram for gram in grams]
    levels = [jnp.sqrt(jnp.sum(system * system, keepdims=True)) for system in systems]
    approach = [system / level for system, level in zip(systems, levels)]
    inverse_root = [None] * len(grams)
    for sweep in range(ITERS):
        if sweep == 0:
            factor = [1.5 * identity - 0.5 * a for a in approach]
        else:
            factor = [1.5 * identity - 0.5 * product(r, a) for r, a in zip(inverse_root, approach)]
        if sweep < ITERS - 1:
            approach = [product(a, f) for a, f in zip(approach, factor)]
        inverse_root = factor if sweep == 0 else [product(f, r) for f, r in zip(factor, inverse_root)]
    result = []
    for inverse, level, projected in zip(inverse_root, levels, projections):
        root = inverse / jnp.sqrt(level)
        wide = jnp.broadcast_to(projected, (8, size))
        mean_shift = product(product(wide, root), root)[:1]
        result.append((math.sqrt(size - 1) * root + mean_shift).astype(BF16))
    return result


def kernel(
    nx, nz, ncell,
    x_ref, y_any, d_any, e_any, idx_any, tally_any, loc_any,
    out_ref,
    arrived, result, grams, sums_out, sums_in, sums_own, stats, partial, cells, flat, change, dep, prec,
    y_ref, d_ref, e_ref, locs, idx_ref, tally_ref, loc_ref,
    in_send, in_recv, in_self, small_send, small_recv, z_send, z_recv, x_send, x_recv,
    out_send, out_recv, out_self, load,
):
    n = nx * nz
    me, cell = lax.axis_index("mem"), lax.axis_index("cell")
    my_x, my_z = me // nz, me % nz
    patches, _, rows, points = arrived.shape
    blocks, obs, members = y_ref.shape
    half = members // 2
    nlist = loc_ref.shape[2]
    line = nz * blocks

    def peer(dx, dz):
        return lax.rem(my_x + dx + nx, nx) * nz + lax.rem(my_z + dz + nz, nz)

    def remote(src, dst, ssem, rsem, to):
        return pltpu.make_async_remote_copy(
            src_ref=src, dst_ref=dst, send_sem=ssem, recv_sem=rsem, device_id=to, device_id_type=MESH
        )

    def to_all(make):
        @pl.loop(1, n)
        def _(o):
            make(peer(o // nz, o % nz)).start()

    barrier = pltpu.get_barrier_semaphore()

    @pl.loop(1, n)
    def _(o):
        pl.semaphore_signal(barrier, inc=1, device_id={"mem": peer(o // nz, o % nz)}, device_id_type=MESH)

    @pl.loop(1, ncell)
    def _(o):
        pl.semaphore_signal(barrier, inc=1, device_id={"cell": lax.rem(cell + o, ncell)}, device_id_type=MESH)

    loads = [
        pltpu.make_async_copy(src, dst, load.at[k])
        for k, (src, dst) in enumerate(
            [(y_any, y_ref), (d_any, d_ref), (e_any, e_ref), (loc_any, locs.at[my_x]), (idx_any, idx_ref), (tally_any, tally_ref)]
        )
    ]
    for copy in loads:
        copy.start()

    pl.semaphore_wait(barrier, n - 1 + ncell - 1)

    def columns(owner, p):
        return pl.ds(pl.multiple_of((owner * patches + p) * points, 128), points)

    def own_in(p):
        return pltpu.make_async_copy(x_ref.at[:, columns(me, p)], arrived.at[p, me], in_self.at[p])

    batches = [(p, first) for p in range(patches) for first in range(1, n, BATCH)]
    sent, left = [], []

    def wait_in_send(k):
        p, first = batches[k]
        size = min(BATCH, n - first)
        ref = arrived.at[p, pl.ds(0, size)]
        remote(ref, ref, in_send.at[k], in_recv.at[p], {"mem": me}).wait_send()

    def pump(count=len(batches), window=WINDOW):
        for k in range(len(sent), min(len(sent) + count, len(batches))):
            p, first = batches[k]
            if k >= window:
                wait_in_send(k - window)
                left.append(k - window)
            if first == 1:
                own_in(p).start()

            @pl.loop(first, min(first + BATCH, n))
            def _(o):
                r = peer(o // nz, o % nz)
                remote(
                    x_ref.at[:, columns(r, p)], arrived.at[p, me], in_send.at[k], in_recv.at[p], {"mem": r}
                ).start()

            sent.append(k)

    pump(WINDOW)

    loads[3].wait()
    for dx in range(1, nx):
        ref = locs.at[my_x]
        remote(ref, ref, small_send.at[2], small_recv.at[2], {"mem": peer(dx, 0)}).start()
    for copy in loads[:3]:
        copy.wait()

    dep[...] = d_ref[...].astype(F32)
    prec[...] = e_ref[...].astype(F32)
    lane = iota((1, members), 1)
    diagonal_mask = iota((members, members), 0) == iota((members, members), 1)

    def one_block(b, tallied):
        y = y_ref[b]
        e, d = prec[pl.ds(b, 1), :], dep[pl.ds(b, 1), :]
        weighted = (y.astype(F32).T * e).astype(BF16)
        gram = jnp.dot(weighted, y, preferred_element_type=F32)
        high, low = split(e * d)
        row = iota((16, obs), 0)
        pair = jnp.where(row == 0, high.astype(F32), jnp.where(row == 1, low.astype(F32), 0.0)).astype(BF16)
        projected = jnp.sum(jnp.dot(pair, y, preferred_element_type=F32), axis=0, keepdims=True)
        diagonal = jnp.sum(jnp.where(diagonal_mask, gram, 0.0), axis=0, keepdims=True)
        grams[my_z * blocks + b] = with_tail(fold(gram), diagonal, projected)
        power = jnp.sum(e * d * d, keepdims=True)
        spread = jnp.sum(diagonal, keepdims=True)
        return tallied + jnp.where(lane == b, power, 0.0) + jnp.where(lane == blocks + b, spread, 0.0)

    stats[me] = lax.fori_loop(0, blocks, one_block, jnp.zeros((1, members), F32))

    def small_copy(which, buffer, place, to):
        return remote(buffer.at[place], buffer.at[place], small_send.at[which], small_recv.at[which], to)

    def wait_small(which, buffer):
        whole = buffer.at[pl.ds(0, buffer.shape[0] - 1)]
        remote(whole, whole, small_send.at[which], small_recv.at[which], {"mem": me}).wait()

    to_all(lambda r: small_copy(3, stats, me, {"mem": r}))

    first, second = (0, blocks // 2), (blocks // 2, blocks // 2)

    def along_z(shift, part, sem, step):
        start, size = part or (0, blocks)
        ref = grams.at[pl.ds(lax.rem(my_z + shift + nz, nz) * blocks + start, size)]
        return remote(ref, ref, z_send.at[sem], z_recv.at[sem], {"mem": peer(0, step)})

    reach = nz // 2

    def forward(step):
        last = step == reach - 1
        for block in range(blocks):
            if not last or block < blocks // 2:
                along_z(-step, (block, 1), step, 1).start()
            if not last or block >= blocks // 2:
                along_z(step, (block, 1), reach + step, -1).start()

    def receive(step):
        last = step == reach
        along_z(-step, first if last else None, step - 1, 1).wait_recv()
        along_z(step, second if last else None, reach + step - 1, -1).wait_recv()

    forward(0)
    loads[4].wait()
    loads[5].wait()
    wait_small(2, locs)
    to_scalar = pltpu.make_async_copy(locs, loc_ref, load.at[6])
    to_scalar.start()
    to_scalar.wait()

    def weight(x, p, s):
        active = jnp.clip(tally_ref[0, (x * nz + my_z) * patches + p] - s, 0, 1).astype(F32)
        return loc_ref[x, p, s] * active

    def listed(x, p, s):
        return idx_ref[s, (x * nz + my_z) * patches + p]

    pump(PACE)

    def add_request(p, total):
        for s in range(nlist):
            far = jnp.abs(block_at - listed(my_x, p, s))
            total = total + weight(my_x, p, s) * (1 - jnp.minimum(far, 1)).astype(F32)
        return total

    row, column = iota((n, members), 0), iota((n, members), 1)
    block_at = jnp.where(column < 2 * blocks, row * blocks + column % blocks, -1)
    asked = lax.fori_loop(0, patches, add_request, jnp.zeros((n, members), F32))
    wait_small(3, stats)
    shares = asked * jnp.sum(stats[...], axis=1)
    partial[me] = jnp.sum(shares, axis=0, keepdims=True)
    to_all(lambda r: small_copy(0, partial, me, {"mem": r}))
    receive(1)
    forward(1)
    pump(PACE)

    wait_small(0, partial)
    cells[cell] = jnp.sum(partial[...], axis=0)

    @pl.loop(1, ncell)
    def _(o):
        small_copy(1, cells, cell, {"cell": lax.rem(cell + o, ncell)}).start()

    for step in range(2, reach):
        receive(step)
        forward(step)
        pump(PACE)
    receive(reach)

    def add_blocks(dx):
        x = lax.rem(my_x + dx, nx)

        @pl.loop(0, patches)
        def _(p):
            total = jnp.zeros(grams.shape[1:], F32)
            for s in range(nlist):
                blk = listed(x, p, s)
                far = jnp.abs((blk >> (line.bit_length() - 1)) - my_x)
                w = weight(x, p, s) * (1 - jnp.minimum(far, 1)).astype(F32)
                total = total + w * grams[blk & (line - 1)].astype(F32)
            if dx:
                sums_out[dx - 1, p] = with_tail(*from_tail(total))
                remote(
                    sums_out.at[dx - 1, p], sums_in.at[dx - 1, p], x_send.at[0], x_recv.at[0], {"mem": peer(dx, 0)}
                ).start()
            else:
                sums_own[p] = total

    for dx in range(1, nx):
        add_blocks(dx)
    add_blocks(0)
    pump(PACE)
    remote(sums_in, sums_in, x_send.at[0], x_recv.at[0], {"mem": me}).wait()

    wait_small(1, cells)
    sums = jnp.sum(cells[...], axis=0)
    power = jnp.sum(jnp.where(lane < blocks, sums, 0.0), keepdims=True)
    spread = jnp.sum(jnp.where((lane >= blocks) & (lane < 2 * blocks), sums, 0.0), keepdims=True) / (members - 1)
    ridge = (members - 1) / (power / spread)

    for step in range(reach):
        last = step == reach - 1
        along_z(-step, first if last else None, step, 1).wait_send()
        along_z(step, second if last else None, reach + step, -1).wait_send()

    pump(window=len(batches))

    def collect(p):
        total = sums_own[p]
        for k in range(nx - 1):
            total = total + sums_in[k, p].astype(F32)
        gram, diagonal, projected = from_tail(total)
        return unfold(gram, diagonal), projected

    @pl.loop(0, patches // GROUP)
    def _(g):
        pairs = [collect(g * GROUP + k) for k in range(GROUP)]
        made = transforms([a for a, _ in pairs], [b for _, b in pairs], ridge)
        for k in range(GROUP):
            change[g * GROUP + k] = made[k]

    @pl.loop(0, patches)
    def _(p):
        whole = arrived.at[p, pl.ds(0, n - 1)]
        remote(whole, whole, in_send.at[p], in_recv.at[p], {"mem": me}).wait_recv()
        own_in(p).wait()

        @pl.loop(0, points // CHUNK)
        def _(c):
            cut = pl.ds(pl.multiple_of(c * CHUNK, CHUNK), CHUNK)
            for m in range(n):
                flat[rows * m : rows * (m + 1), :] = arrived[p, m, :, cut].astype(F32)
            states = flat[...]
            means = jnp.sum(states, axis=0, keepdims=True) * (1.0 / members)
            deviation = (states - means).astype(BF16)
            updated = means + jnp.dot(change[p], deviation, preferred_element_type=F32)
            for m in range(n):
                result[p, m, :, cut] = updated[rows * m : rows * (m + 1), :].astype(BF16)

        pltpu.make_async_copy(result.at[p, me], out_ref.at[:, columns(me, p)], out_self.at[0]).start()
        to_all(
            lambda r: remote(
                result.at[p, r], out_ref.at[:, columns(me, p)], out_send.at[0], out_recv.at[0], {"mem": r}
            )
        )

    for k in range(len(left), len(batches)):
        wait_in_send(k)
    mine_out = pl.ds(pl.multiple_of(me * patches * points, 128), patches * points)
    pltpu.make_async_copy(out_ref.at[:, mine_out], out_ref.at[:, mine_out], out_self.at[0]).wait()
    others = out_ref.at[:, pl.ds(0, (n - 1) * patches * points)]
    remote(others, others, out_send.at[0], out_recv.at[0], {"mem": me}).wait()


def body(nx, nz, ncell, prior_states, anomalies, departure, precision, lists, tallies, localization):
    n = nx * nz
    rows, cells = prior_states.shape
    patches, nlist = localization.shape[1:]
    points = cells // (n * patches)
    blocks, obs, members = anomalies.shape[1:]
    anywhere = pl.BlockSpec(memory_space=pl.ANY)
    dma = pltpu.SemaphoreType.DMA
    return pl.pallas_call(
        functools.partial(kernel, nx, nz, ncell),
        out_shape=pltpu.VMEM((rows, cells), BF16),
        in_specs=[anywhere] * 7,
        out_specs=anywhere,
        scratch_shapes=[
            pltpu.VMEM((patches, n, rows, points), BF16),
            pltpu.VMEM((patches, n, rows, points), BF16),
            pltpu.VMEM((n // nx * blocks, members // 2 + 8, members), BF16),
            pltpu.VMEM((nx - 1, patches, members // 2 + 8, members), BF16),
            pltpu.VMEM((nx - 1, patches, members // 2 + 8, members), BF16),
            pltpu.VMEM((patches, members // 2 + 8, members), F32),
            pltpu.VMEM((n, 1, members), F32),
            pltpu.VMEM((n, 1, members), F32),
            pltpu.VMEM((ncell, 1, members), F32),
            pltpu.VMEM((members, CHUNK), F32),
            pltpu.VMEM((patches, members, members), BF16),
            pltpu.VMEM((blocks, obs), F32),
            pltpu.VMEM((blocks, obs), F32),
            pltpu.VMEM((blocks, obs, members), BF16),
            pltpu.VMEM((blocks, obs), BF16),
            pltpu.VMEM((blocks, obs), BF16),
            pltpu.VMEM((nx, patches, nlist), F32),
            pltpu.SMEM((nlist, lists.shape[1]), jnp.int32),
            pltpu.SMEM((1, lists.shape[1]), jnp.int32),
            pltpu.SMEM((nx, patches, nlist), F32),
            dma((patches * (-(-(n - 1) // BATCH)),)),
            dma((patches,)),
            dma((patches,)),
            dma((4,)),
            dma((4,)),
            dma((nz,)),
            dma((nz,)),
            dma((1,)),
            dma((1,)),
            dma((1,)),
            dma((1,)),
            dma((1,)),
            dma((7,)),
        ],
        compiler_params=pltpu.CompilerParams(
            collective_id=0, has_side_effects=True, vmem_limit_bytes=20 * 2**20
        ),
        name="analysis_kernel",
    )(
        *(
            pltpu.with_memory_space_constraint(operand, pltpu.HBM)
            for operand in (
                prior_states, anomalies[0], departure[0], precision[0], lists[0].T, tallies, localization[0]
            )
        )
    )


def solution(mesh):
    nx, nz = 4, mesh.shape["mem"] // 4
    return jax.shard_map(
        functools.partial(body, nx, nz, mesh.shape["cell"]),
        mesh=mesh,
        in_specs=(
            P("mem", "cell"),
            P("cell", "mem", None, None),
            P("cell", "mem", None),
            P("cell", "mem", None),
            P("cell", None, None),
            P("cell", None),
            P("cell", "mem", None),
        ),
        out_specs=P("mem", "cell"),
        check_vma=False,
    )
```

time: 231 us -> 207 us (0.90)
  Pallas kernels: 220 us -> 204 us
  local copies, waits for them, and re-layouts: 8.66 us -> 2.02 us
    pallas_call x1, Pallas kernels: 220 us -> 204 us  [body(): pl.pallas_call(functools.partial(kernel, nx, nz, ncell), out_shape=pltpu....]
    unnamed x3 -> x1, local copies, waits for them, and re-layouts: 5.29 us -> 2.02 us
where the time goes in v2:
time: 207 us; the launch traced here: 206 us
  Pallas kernels  204 us (99%)
    pallas_call x1, Pallas kernels, body(): pl.pallas_call(functools.partial(kernel, nx, nz, ncell), out_shape=pltpu....  204 us

profile of v2, /device:TPU:2, one launch (start us, length us, event | category | flops | bytes accessed | tf_op | source)
XLA Modules:
  0.0 206.5 jit_solution(12864087876597856814)
XLA Ops:
  0.0 204.4 %analysis_kernel.1 = bf16[4,524288]{1,0:T(4,128)(2,1)S(1)} custom-call(bf16[4,524288]{1,0:T(4,128)(2,1)} %x_ref.1, bf16[8,256,128]{2,1,0:T(8,128)(2,1)} %bitcast.7, bf16[8,256]{1,0:T(8,128)(2,1)} %bitcast.9, bf16[8,256]{1,0:T(8,128)(2,1)} %bitcast.10, s32[8,256]{1,0:T(8,128)} %bitcast.8, s32[1,256]{1,0:T(1,128)} %tally_any.1, f32[8,8]{1,0:T(8,128)} %bitcast.11), custom_call_target="tpu_custom_call" | custom-call | tf_op jit(solution)/shard_map/analysis_kernel/pallas_call | solution.py:375
  204.4 2.0 copy.9

commit v3 on v2

--- a/solution.py
+++ b/solution.py
@@ -89,9 +89,9 @@
     nx, nz, ncell,
     x_ref, y_any, d_any, e_any, idx_any, tally_any, loc_any,
     out_ref,
-    arrived, result, grams, sums_out, sums_in, sums_own, stats, partial, cells, flat, change, dep, prec,
+    arrived, result, grams, sums_out, sums_in, sums_own, stats, partial, cells, flat, change, dep, prec, lines, tails,
     y_ref, d_ref, e_ref, locs, idx_ref, tally_ref, loc_ref,
-    in_send, in_recv, in_self, small_send, small_recv, z_send, z_recv, x_send, x_recv,
+    in_send, in_recv, in_self, small_send, small_recv, z_send, z_recv, tail_send, tail_recv, x_send, x_recv,
     out_send, out_recv, out_self, load,
 ):
     n = nx * nz
@@ -111,19 +111,20 @@
             src_ref=src, dst_ref=dst, send_sem=ssem, recv_sem=rsem, device_id=to, device_id_type=MESH
         )
 
+    def partner(o):
+        turned = o + (cell % 2) * (n - 2 * o)
+        return peer(turned // nz, turned % nz)
+
     def to_all(make):
         @pl.loop(1, n)
         def _(o):
-            make(peer(o // nz, o % nz)).start()
+            make(partner(o)).start()
 
     barrier = pltpu.get_barrier_semaphore()
 
-    @pl.loop(1, n)
-    def _(o):
-        pl.semaphore_signal(barrier, inc=1, device_id={"mem": peer(o // nz, o % nz)}, device_id_type=MESH)
-
-    @pl.loop(1, ncell)
-    def _(o):
+    for o in range(1, n):
+        pl.semaphore_signal(barrier, inc=1, device_id={"mem": lax.rem(me + o, n)}, device_id_type=MESH)
+    for o in range(1, ncell):
         pl.semaphore_signal(barrier, inc=1, device_id={"cell": lax.rem(cell + o, ncell)}, device_id_type=MESH)
 
     loads = [
@@ -163,7 +164,7 @@
 
             @pl.loop(first, min(first + BATCH, n))
             def _(o):
-                r = peer(o // nz, o % nz)
+                r = partner(o)
                 remote(
                     x_ref.at[:, columns(r, p)], arrived.at[p, me], in_send.at[k], in_recv.at[p], {"mem": r}
                 ).start()
@@ -194,12 +195,15 @@
         pair = jnp.where(row == 0, high.astype(F32), jnp.where(row == 1, low.astype(F32), 0.0)).astype(BF16)
         projected = jnp.sum(jnp.dot(pair, y, preferred_element_type=F32), axis=0, keepdims=True)
         diagonal = jnp.sum(jnp.where(diagonal_mask, gram, 0.0), axis=0, keepdims=True)
-        grams[my_z * blocks + b] = with_tail(fold(gram), diagonal, projected)
+        grams[my_z * blocks + b] = fold(gram).astype(BF16)
+        lines[pl.ds(b, 1), :] = diagonal
+        lines[pl.ds(blocks + b, 1), :] = projected
         power = jnp.sum(e * d * d, keepdims=True)
         spread = jnp.sum(diagonal, keepdims=True)
         return tallied + jnp.where(lane == b, power, 0.0) + jnp.where(lane == blocks + b, spread, 0.0)
 
     stats[me] = lax.fori_loop(0, blocks, one_block, jnp.zeros((1, members), F32))
+    tails[my_z] = lines[...].astype(BF16)
 
     def small_copy(which, buffer, place, to):
         return remote(buffer.at[place], buffer.at[place], small_send.at[which], small_recv.at[which], to)
@@ -217,10 +221,17 @@
         ref = grams.at[pl.ds(lax.rem(my_z + shift + nz, nz) * blocks + start, size)]
         return remote(ref, ref, z_send.at[sem], z_recv.at[sem], {"mem": peer(0, step)})
 
+    def tail_along_z(shift, sem, step):
+        ref = tails.at[lax.rem(my_z + shift + nz, nz)]
+        return remote(ref, ref, tail_send.at[sem], tail_recv.at[sem], {"mem": peer(0, step)})
+
     reach = nz // 2
 
     def forward(step):
         last = step == reach - 1
+        tail_along_z(-step, step, 1).start()
+        if not last:
+            tail_along_z(step, reach + step, -1).start()
         for block in range(blocks):
             if not last or block < blocks // 2:
                 along_z(-step, (block, 1), step, 1).start()
@@ -229,6 +240,9 @@
 
     def receive(step):
         last = step == reach
+        tail_along_z(-step, step - 1, 1).wait_recv()
+        if not last:
+            tail_along_z(step, reach + step - 1, -1).wait_recv()
         along_z(-step, first if last else None, step - 1, 1).wait_recv()
         along_z(step, second if last else None, reach + step - 1, -1).wait_recv()
 
@@ -279,24 +293,31 @@
         pump(PACE)
     receive(reach)
 
+    in_page = iota(lines.shape, 0) % blocks
+
     def add_blocks(dx):
         x = lax.rem(my_x + dx, nx)
 
         @pl.loop(0, patches)
         def _(p):
-            total = jnp.zeros(grams.shape[1:], F32)
+            total, rest = jnp.zeros(grams.shape[1:], F32), jnp.zeros(lines.shape, F32)
             for s in range(nlist):
                 blk = listed(x, p, s)
                 far = jnp.abs((blk >> (line.bit_length() - 1)) - my_x)
                 w = weight(x, p, s) * (1 - jnp.minimum(far, 1)).astype(F32)
-                total = total + w * grams[blk & (line - 1)].astype(F32)
+                place = blk & (line - 1)
+                total = total + w * grams[place].astype(F32)
+                hot = 1 - jnp.minimum(jnp.abs(in_page - (place & (blocks - 1))), 1)
+                rest = rest + (w * hot.astype(F32)) * tails[place >> (blocks.bit_length() - 1)].astype(F32)
+            diagonal = jnp.sum(rest[:blocks], axis=0, keepdims=True)
+            projected = jnp.sum(rest[blocks:], axis=0, keepdims=True)
             if dx:
-                sums_out[dx - 1, p] = with_tail(*from_tail(total))
+                sums_out[dx - 1, p] = with_tail(total, diagonal, projected)
                 remote(
                     sums_out.at[dx - 1, p], sums_in.at[dx - 1, p], x_send.at[0], x_recv.at[0], {"mem": peer(dx, 0)}
                 ).start()
             else:
-                sums_own[p] = total
+                sums_own[p] = jnp.concatenate([total, diagonal, jnp.zeros_like(diagonal), projected, jnp.zeros((5, members), F32)], axis=0)
 
     for dx in range(1, nx):
         add_blocks(dx)
@@ -312,6 +333,9 @@
 
     for step in range(reach):
         last = step == reach - 1
+        tail_along_z(-step, step, 1).wait_send()
+        if not last:
+            tail_along_z(step, reach + step, -1).wait_send()
         along_z(-step, first if last else None, step, 1).wait_send()
         along_z(step, second if last else None, reach + step, -1).wait_send()
 
@@ -380,7 +404,7 @@
         scratch_shapes=[
             pltpu.VMEM((patches, n, rows, points), BF16),
             pltpu.VMEM((patches, n, rows, points), BF16),
-            pltpu.VMEM((n // nx * blocks, members // 2 + 8, members), BF16),
+            pltpu.VMEM((n // nx * blocks, members // 2, members), BF16),
             pltpu.VMEM((nx - 1, patches, members // 2 + 8, members), BF16),
             pltpu.VMEM((nx - 1, patches, members // 2 + 8, members), BF16),
             pltpu.VMEM((patches, members // 2 + 8, members), F32),
@@ -391,6 +415,8 @@
             pltpu.VMEM((patches, members, members), BF16),
             pltpu.VMEM((blocks, obs), F32),
             pltpu.VMEM((blocks, obs), F32),
+            pltpu.VMEM((2 * blocks, members), F32),
+            pltpu.VMEM((n // nx, 2 * blocks, members), BF16),
             pltpu.VMEM((blocks, obs, members), BF16),
             pltpu.VMEM((blocks, obs), BF16),
             pltpu.VMEM((blocks, obs), BF16),
@@ -403,6 +429,8 @@
             dma((patches,)),
             dma((4,)),
             dma((4,)),
+            dma((nz,)),
+            dma((nz,)),
             dma((nz,)),
             dma((nz,)),
             dma((1,)),

time: 207 us -> 206 us (level)
  no operation moved by 1% of the time
where the time goes in v3:
time: 206 us
  Pallas kernels  204 us (99%)
    pallas_call x1, Pallas kernels, body(): pl.pallas_call(functools.partial(kernel, nx, nz, ncell), out_shape=pltpu....  204 us

profile of v3, /device:TPU:2, one launch (start us, length us, event | category | flops | bytes accessed | tf_op | source)
XLA Modules:
  0.0 205.7 jit_solution(9982042854976756433)
XLA Ops:
  0.0 203.6 %analysis_kernel.1 = bf16[4,524288]{1,0:T(4,128)(2,1)S(1)} custom-call(bf16[4,524288]{1,0:T(4,128)(2,1)} %x_ref.1, bf16[8,256,128]{2,1,0:T(8,128)(2,1)} %bitcast.7, bf16[8,256]{1,0:T(8,128)(2,1)} %bitcast.9, bf16[8,256]{1,0:T(8,128)(2,1)} %bitcast.10, s32[8,256]{1,0:T(8,128)} %bitcast.8, s32[1,256]{1,0:T(1,128)} %tally_any.1, f32[8,8]{1,0:T(8,128)} %bitcast.11), custom_call_target="tpu_custom_call" | custom-call | tf_op jit(solution)/shard_map/analysis_kernel/pallas_call | solution.py:399
  203.6 2.0 copy.9

commit v4 on v3

--- a/solution.py
+++ b/solution.py
@@ -203,7 +203,8 @@
         return tallied + jnp.where(lane == b, power, 0.0) + jnp.where(lane == blocks + b, spread, 0.0)
 
     stats[me] = lax.fori_loop(0, blocks, one_block, jnp.zeros((1, members), F32))
-    tails[my_z] = lines[...].astype(BF16)
+    pairs = split(lines[:blocks, :]) + split(lines[blocks:, :])
+    tails[my_z] = jnp.concatenate([part.astype(F32) for part in pairs], axis=0).astype(BF16)
 
     def small_copy(which, buffer, place, to):
         return remote(buffer.at[place], buffer.at[place], small_send.at[which], small_recv.at[which], to)
@@ -293,14 +294,14 @@
         pump(PACE)
     receive(reach)
 
-    in_page = iota(lines.shape, 0) % blocks
+    in_page = iota(tails.shape[1:], 0) % blocks
 
     def add_blocks(dx):
         x = lax.rem(my_x + dx, nx)
 
         @pl.loop(0, patches)
         def _(p):
-            total, rest = jnp.zeros(grams.shape[1:], F32), jnp.zeros(lines.shape, F32)
+            total, rest = jnp.zeros(grams.shape[1:], F32), jnp.zeros(tails.shape[1:], F32)
             for s in range(nlist):
                 blk = listed(x, p, s)
                 far = jnp.abs((blk >> (line.bit_length() - 1)) - my_x)
@@ -309,15 +310,16 @@
                 total = total + w * grams[place].astype(F32)
                 hot = 1 - jnp.minimum(jnp.abs(in_page - (place & (blocks - 1))), 1)
                 rest = rest + (w * hot.astype(F32)) * tails[place >> (blocks.bit_length() - 1)].astype(F32)
-            diagonal = jnp.sum(rest[:blocks], axis=0, keepdims=True)
-            projected = jnp.sum(rest[blocks:], axis=0, keepdims=True)
+            diagonal = jnp.sum(rest[: 2 * blocks], axis=0, keepdims=True)
+            projected = jnp.sum(rest[2 * blocks :], axis=0, keepdims=True)
             if dx:
                 sums_out[dx - 1, p] = with_tail(total, diagonal, projected)
                 remote(
                     sums_out.at[dx - 1, p], sums_in.at[dx - 1, p], x_send.at[0], x_recv.at[0], {"mem": peer(dx, 0)}
                 ).start()
             else:
-                sums_own[p] = jnp.concatenate([total, diagonal, jnp.zeros_like(diagonal), projected, jnp.zeros((5, members), F32)], axis=0)
+                none = jnp.zeros_like(diagonal)
+                sums_own[p] = jnp.concatenate([total, diagonal, none, projected] + [none] * 5, axis=0)
 
     for dx in range(1, nx):
         add_blocks(dx)
@@ -416,7 +418,7 @@
             pltpu.VMEM((blocks, obs), F32),
             pltpu.VMEM((blocks, obs), F32),
             pltpu.VMEM((2 * blocks, members), F32),
-            pltpu.VMEM((n // nx, 2 * blocks, members), BF16),
+            pltpu.VMEM((n // nx, 4 * blocks, members), BF16),
             pltpu.VMEM((blocks, obs, members), BF16),
             pltpu.VMEM((blocks, obs), BF16),
             pltpu.VMEM((blocks, obs), BF16),

time: 206 us -> 206 us (level)
  no operation moved by 1% of the time
where the time goes in v4:
time: 206 us
  Pallas kernels  204 us (99%)
    pallas_call x1, Pallas kernels, body(): pl.pallas_call(functools.partial(kernel, nx, nz, ncell), out_shape=pltpu....  204 us

profile of v4, /device:TPU:2, one launch (start us, length us, event | category | flops | bytes accessed | tf_op | source)
XLA Modules:
  0.0 206.0 jit_solution(16498880174528522899)
XLA Ops:
  0.0 204.0 %analysis_kernel.1 = bf16[4,524288]{1,0:T(4,128)(2,1)S(1)} custom-call(bf16[4,524288]{1,0:T(4,128)(2,1)} %x_ref.1, bf16[8,256,128]{2,1,0:T(8,128)(2,1)} %bitcast.7, bf16[8,256]{1,0:T(8,128)(2,1)} %bitcast.9, bf16[8,256]{1,0:T(8,128)(2,1)} %bitcast.10, s32[8,256]{1,0:T(8,128)} %bitcast.8, s32[1,256]{1,0:T(1,128)} %tally_any.1, f32[8,8]{1,0:T(8,128)} %bitcast.11), custom_call_target="tpu_custom_call" | custom-call | tf_op jit(solution)/shard_map/analysis_kernel/pallas_call | solution.py:401
  204.0 2.0 copy.9

commit v5 on v4

--- a/solution.py
+++ b/solution.py
@@ -89,7 +89,7 @@
     nx, nz, ncell,
     x_ref, y_any, d_any, e_any, idx_any, tally_any, loc_any,
     out_ref,
-    arrived, result, grams, sums_out, sums_in, sums_own, stats, partial, cells, flat, change, dep, prec, lines, tails,
+    arrived, result, grams, sums_out, sums_in, sums_own, stats, partial, line_sums, cells, flat, change, dep, prec, lines, tails,
     y_ref, d_ref, e_ref, locs, idx_ref, tally_ref, loc_ref,
     in_send, in_recv, in_self, small_send, small_recv, z_send, z_recv, tail_send, tail_recv, x_send, x_recv,
     out_send, out_recv, out_self, load,
@@ -114,11 +114,6 @@
     def partner(o):
         turned = o + (cell % 2) * (n - 2 * o)
         return peer(turned // nz, turned % nz)
-
-    def to_all(make):
-        @pl.loop(1, n)
-        def _(o):
-            make(partner(o)).start()
 
     barrier = pltpu.get_barrier_semaphore()
 
@@ -209,11 +204,12 @@
     def small_copy(which, buffer, place, to):
         return remote(buffer.at[place], buffer.at[place], small_send.at[which], small_recv.at[which], to)
 
-    def wait_small(which, buffer):
-        whole = buffer.at[pl.ds(0, buffer.shape[0] - 1)]
+    def wait_small(which, buffer, count):
+        whole = buffer.at[pl.ds(0, count)]
         remote(whole, whole, small_send.at[which], small_recv.at[which], {"mem": me}).wait()
 
-    to_all(lambda r: small_copy(3, stats, me, {"mem": r}))
+    for dz in range(1, nz):
+        small_copy(3, stats, me, {"mem": peer(0, dz)}).start()
 
     first, second = (0, blocks // 2), (blocks // 2, blocks // 2)
 
@@ -250,7 +246,7 @@
     forward(0)
     loads[4].wait()
     loads[5].wait()
-    wait_small(2, locs)
+    wait_small(2, locs, nx - 1)
     to_scalar = pltpu.make_async_copy(locs, loc_ref, load.at[6])
     to_scalar.start()
     to_scalar.wait()
@@ -273,25 +269,39 @@
     row, column = iota((n, members), 0), iota((n, members), 1)
     block_at = jnp.where(column < 2 * blocks, row * blocks + column % blocks, -1)
     asked = lax.fori_loop(0, patches, add_request, jnp.zeros((n, members), F32))
-    wait_small(3, stats)
-    shares = asked * jnp.sum(stats[...], axis=1)
-    partial[me] = jnp.sum(shares, axis=0, keepdims=True)
-    to_all(lambda r: small_copy(0, partial, me, {"mem": r}))
+    my_line = pl.ds(my_x * nz, nz)
+    wait_small(3, stats, nz - 1)
+    for dx in range(1, nx):
+        small_copy(4, stats, my_line, {"mem": peer(dx, 0)}).start()
     receive(1)
     forward(1)
     pump(PACE)
 
-    wait_small(0, partial)
-    cells[cell] = jnp.sum(partial[...], axis=0)
+    wait_small(4, stats, (nx - 1) * nz)
+    shares = asked * jnp.sum(stats[...], axis=1)
+    partial[my_z] = jnp.sum(shares, axis=0, keepdims=True)
+    for dz in range(1, nz):
+        small_copy(0, partial, my_z, {"mem": peer(0, dz)}).start()
+    receive(2)
+    forward(2)
+    pump(PACE)
+
+    wait_small(0, partial, nz - 1)
+    line_sums[my_x] = jnp.sum(partial[...], axis=0)
+    for dx in range(1, nx):
+        small_copy(5, line_sums, my_x, {"mem": peer(dx, 0)}).start()
+    for step in range(3, reach):
+        receive(step)
+        forward(step)
+        pump(PACE)
+
+    wait_small(5, line_sums, nx - 1)
+    cells[cell] = jnp.sum(line_sums[...], axis=0)
 
     @pl.loop(1, ncell)
     def _(o):
         small_copy(1, cells, cell, {"cell": lax.rem(cell + o, ncell)}).start()
 
-    for step in range(2, reach):
-        receive(step)
-        forward(step)
-        pump(PACE)
     receive(reach)
 
     in_page = iota(tails.shape[1:], 0) % blocks
@@ -327,7 +337,7 @@
     pump(PACE)
     remote(sums_in, sums_in, x_send.at[0], x_recv.at[0], {"mem": me}).wait()
 
-    wait_small(1, cells)
+    wait_small(1, cells, ncell - 1)
     sums = jnp.sum(cells[...], axis=0)
     power = jnp.sum(jnp.where(lane < blocks, sums, 0.0), keepdims=True)
     spread = jnp.sum(jnp.where((lane >= blocks) & (lane < 2 * blocks), sums, 0.0), keepdims=True) / (members - 1)
@@ -376,11 +386,15 @@
                 result[p, m, :, cut] = updated[rows * m : rows * (m + 1), :].astype(BF16)
 
         pltpu.make_async_copy(result.at[p, me], out_ref.at[:, columns(me, p)], out_self.at[0]).start()
-        to_all(
-            lambda r: remote(
-                result.at[p, r], out_ref.at[:, columns(me, p)], out_send.at[0], out_recv.at[0], {"mem": r}
-            )
-        )
+        @pl.loop(0, n)
+        def _(q):
+            r = lax.rem(my_x + q % nx, nx) * nz + (q // (2 * nx)) * 2 + lax.rem(my_z + (q // nx) % 2, 2)
+
+            @pl.when(r != me)
+            def _():
+                remote(
+                    result.at[p, r], out_ref.at[:, columns(me, p)], out_send.at[0], out_recv.at[0], {"mem": r}
+                ).start()
 
     for k in range(len(left), len(batches)):
         wait_in_send(k)
@@ -411,7 +425,8 @@
             pltpu.VMEM((nx - 1, patches, members // 2 + 8, members), BF16),
             pltpu.VMEM((patches, members // 2 + 8, members), F32),
             pltpu.VMEM((n, 1, members), F32),
-            pltpu.VMEM((n, 1, members), F32),
+            pltpu.VMEM((n // nx, 1, members), F32),
+            pltpu.VMEM((nx, 1, members), F32),
             pltpu.VMEM((ncell, 1, members), F32),
             pltpu.VMEM((members, CHUNK), F32),
             pltpu.VMEM((patches, members, members), BF16),
@@ -429,8 +444,8 @@
             dma((patches * (-(-(n - 1) // BATCH)),)),
             dma((patches,)),
             dma((patches,)),
-            dma((4,)),
-            dma((4,)),
+            dma((6,)),
+            dma((6,)),
             dma((nz,)),
             dma((nz,)),
             dma((nz,)),

time: 206 us -> 205 us (level)
  no operation moved by 1% of the time
where the time goes in v5:
time: 205 us; the launch traced here: 204 us
  Pallas kernels  202 us (99%)
    pallas_call x1, Pallas kernels, body(): pl.pallas_call(functools.partial(kernel, nx, nz, ncell), out_shape=pltpu....  202 us

profile of v5, /device:TPU:2, one launch (start us, length us, event | category | flops | bytes accessed | tf_op | source)
XLA Modules:
  0.0 204.0 jit_solution(16400498032716218620)
XLA Ops:
  0.0 202.0 %analysis_kernel.1 = bf16[4,524288]{1,0:T(4,128)(2,1)S(1)} custom-call(bf16[4,524288]{1,0:T(4,128)(2,1)} %x_ref.1, bf16[8,256,128]{2,1,0:T(8,128)(2,1)} %bitcast.7, bf16[8,256]{1,0:T(8,128)(2,1)} %bitcast.9, bf16[8,256]{1,0:T(8,128)(2,1)} %bitcast.10, s32[8,256]{1,0:T(8,128)} %bitcast.8, s32[1,256]{1,0:T(1,128)} %tally_any.1, f32[8,8]{1,0:T(8,128)} %bitcast.11), custom_call_target="tpu_custom_call" | custom-call | tf_op jit(solution)/shard_map/analysis_kernel/pallas_call | solution.py:415
  202.0 2.0 copy.9

commit v6 on v5

--- a/solution.py
+++ b/solution.py
@@ -92,7 +92,7 @@
     arrived, result, grams, sums_out, sums_in, sums_own, stats, partial, line_sums, cells, flat, change, dep, prec, lines, tails,
     y_ref, d_ref, e_ref, locs, idx_ref, tally_ref, loc_ref,
     in_send, in_recv, in_self, small_send, small_recv, z_send, z_recv, tail_send, tail_recv, x_send, x_recv,
-    out_send, out_recv, out_self, load,
+    out_send, out_recv, out_self, load, states_ref,
 ):
     n = nx * nz
     me, cell = lax.axis_index("mem"), lax.axis_index("cell")
@@ -122,6 +122,8 @@
     for o in range(1, ncell):
         pl.semaphore_signal(barrier, inc=1, device_id={"cell": lax.rem(cell + o, ncell)}, device_id_type=MESH)
 
+    whole_states = pltpu.make_async_copy(x_ref, states_ref, load.at[7])
+    whole_states.start()
     loads = [
         pltpu.make_async_copy(src, dst, load.at[k])
         for k, (src, dst) in enumerate(
@@ -132,12 +134,13 @@
         copy.start()
 
     pl.semaphore_wait(barrier, n - 1 + ncell - 1)
+    whole_states.wait()
 
     def columns(owner, p):
         return pl.ds(pl.multiple_of((owner * patches + p) * points, 128), points)
 
     def own_in(p):
-        return pltpu.make_async_copy(x_ref.at[:, columns(me, p)], arrived.at[p, me], in_self.at[p])
+        return pltpu.make_async_copy(states_ref.at[:, columns(me, p)], arrived.at[p, me], in_self.at[p])
 
     batches = [(p, first) for p in range(patches) for first in range(1, n, BATCH)]
     sent, left = [], []
@@ -161,7 +164,7 @@
             def _(o):
                 r = partner(o)
                 remote(
-                    x_ref.at[:, columns(r, p)], arrived.at[p, me], in_send.at[k], in_recv.at[p], {"mem": r}
+                    states_ref.at[:, columns(r, p)], arrived.at[p, me], in_send.at[k], in_recv.at[p], {"mem": r}
                 ).start()
 
             sent.append(k)
@@ -455,7 +458,8 @@
             dma((1,)),
             dma((1,)),
             dma((1,)),
-            dma((7,)),
+            dma((8,)),
+            pltpu.VMEM((rows, cells), BF16),
         ],
         compiler_params=pltpu.CompilerParams(
             collective_id=0, has_side_effects=True, vmem_limit_bytes=20 * 2**20

time: 205 us -> 205 us (level)
  no operation moved by 1% of the time
where the time goes in v6:
time: 205 us; the launch traced here: 204 us
  Pallas kernels  202 us (99%)
    pallas_call x1, Pallas kernels, body(): pl.pallas_call(functools.partial(kernel, nx, nz, ncell), out_shape=pltpu....  202 us

profile of v6, /device:TPU:2, one launch (start us, length us, event | category | flops | bytes accessed | tf_op | source)
XLA Modules:
  0.0 203.8 jit_solution(9409498089839538693)
XLA Ops:
  0.0 201.8 %analysis_kernel.1 = bf16[4,524288]{1,0:T(4,128)(2,1)S(1)} custom-call(bf16[4,524288]{1,0:T(4,128)(2,1)} %x_ref.1, bf16[8,256,128]{2,1,0:T(8,128)(2,1)} %bitcast.7, bf16[8,256]{1,0:T(8,128)(2,1)} %bitcast.9, bf16[8,256]{1,0:T(8,128)(2,1)} %bitcast.10, s32[8,256]{1,0:T(8,128)} %bitcast.8, s32[1,256]{1,0:T(1,128)} %tally_any.1, f32[8,8]{1,0:T(8,128)} %bitcast.11), custom_call_target="tpu_custom_call" | custom-call | tf_op jit(solution)/shard_map/analysis_kernel/pallas_call | solution.py:418
  201.8 2.0 copy.9
